TPU v7x, 128 devices: a whole 4x4x4 slice. The times are simulated.
128 devices in a mesh: dp: 8 (over x_hi, y), fsdp: 16 (over x_lo, z, core).
Axes of the slice: x: 4 (x_hi: 2, x_lo: 2; x = x_hi * 2 + x_lo), y: 4, z: 4, core: 2. Of those that a mesh axis runs over, the one named last changes fastest.
Arguments:
- queries: bfloat16 [16384, 2048], P(('dp', 'fsdp')), may hold values from -16 to 16
- doc_kv: bfloat16 [2, 8, 512, 2048], P(None, 'dp', 'fsdp'), may hold values from -12 to 12
- residual: bfloat16 [16384, 4096], P(('dp', 'fsdp')), may hold values from -25 to 25
- out_weight: bfloat16 [2048, 4096], P(None, 'fsdp'), may hold values from -0.125 to 0.125
- out_gain: float32 [4096], replicated, may hold values from 0.1 to 1.9
- head: bfloat16 [16384, 4096], P('fsdp')
- source: int32 [8], replicated, may hold values from 0 to 7, each once
- lengths: int32 [8, 8], P('dp'), may hold values from 1 to 256, 1280 in all within a row
- sampled: int32 [16384], P(('dp', 'fsdp')), may hold values from 0 to 16383
- old_logprob: float32 [16384], P(('dp', 'fsdp')), may hold values from -13 to -7
Outputs:
- log_ratio: float32 [16384], P(('dp', 'fsdp'))
- kl_term: float32 [16384], P(('dp', 'fsdp'))
Inputs may be any that keep to these rules, and one draw needn't show every extreme that they name: Each row of lengths sums to 1280. `source`: each document appears once.
All inputs are finite; a program needn't handle non-finite values.
Results may differ from a plain program's by a relative error of at most 0.0028.
Values may be sent and summed in bfloat16 or wider, within the bound.
A program may use at most 128 MiB of HBM per device.

v0:
```python
import jax
import jax.numpy as jnp
from jax import lax
from jax.sharding import PartitionSpec as P

HEADS = 8


def joined(value, axis, join):
    pieces = jax.tree.map(lambda part: lax.all_gather(part, axis), value)
    head = jax.tree.map(lambda part: part[0], pieces)
    tail = jax.tree.map(lambda part: part[1:], pieces)
    total, _ = lax.scan(lambda total, share: (join(total, share), None), head, tail)
    return total


def attend(query_rows, keys, values, heads):
    count = query_rows.shape[0]
    width = query_rows.shape[1]
    depth = width // heads
    q3 = query_rows.reshape(count, heads, depth)
    k3 = keys.reshape(keys.shape[0], heads, depth)
    v3 = values.reshape(values.shape[0], heads, depth)
    scores = jnp.einsum("thd,lhd->htl", q3, k3, preferred_element_type=jnp.float32) * float(
        depth
    ) ** (-0.5)
    largest = jnp.max(scores, axis=2, keepdims=True)
    raised = jnp.exp(scores - largest)
    weights = (raised / jnp.sum(raised, axis=2, keepdims=True)).astype(jnp.bfloat16)
    mixed = jnp.einsum("htl,lhd->thd", weights, v3, preferred_element_type=jnp.float32)
    return mixed.reshape(count, width).astype(jnp.bfloat16)


def combine_totals(first, second):
    highest = jnp.maximum(first[0], second[0])
    total = first[1] * jnp.exp(first[0] - highest) + second[1] * jnp.exp(second[0] - highest)
    return (highest, total, first[2] + second[2])


def on_device(
    queries, doc_kv, residual, out_weight, out_gain, head, source, lengths, sampled, old_logprob
):
    shard_pos = lax.axis_index("fsdp")
    row_pos = lax.axis_index("dp")
    tok_rows = queries.shape[0]
    every_doc = lax.all_gather(doc_kv, "dp", axis=1, tiled=True)
    chosen = lax.dynamic_index_in_dim(every_doc, source[row_pos], 1, keepdims=False)
    whole_doc = lax.all_gather(chosen, "fsdp", axis=1, tiled=True)
    attended = attend(queries, whole_doc[0], whole_doc[1], HEADS)
    mixed = jnp.dot(
        attended,
        lax.all_gather(out_weight, "fsdp", axis=1, tiled=True),
        preferred_element_type=jnp.float32,
    )
    summed = mixed + residual.astype(jnp.float32)
    scale = lax.rsqrt(jnp.mean(summed * summed, axis=1, keepdims=True) + 1e-06)
    hidden = (summed * scale * out_gain[None, :]).astype(jnp.bfloat16)
    group_hidden, group_ids = (
        lax.all_gather(hidden, "fsdp", axis=0, tiled=True),
        lax.all_gather(sampled, "fsdp", axis=0, tiled=True),
    )
    vocab_rows = head.shape[0]
    logits = lax.dot_general(
        group_hidden, head, (((1,), (1,)), ((), ())), preferred_element_type=jnp.float32
    )
    columns = jnp.arange(vocab_rows, dtype=jnp.int32) + shard_pos * vocab_rows
    matches = columns[None, :] == group_ids[:, None]
    picked = jnp.sum(jnp.where(matches, logits, 0.0), axis=1)
    largest = jnp.max(logits, axis=1)
    own_start = shard_pos * tok_rows
    total = jnp.sum(jnp.exp(logits - largest[:, None]), axis=1)
    highest, total, picked = joined((largest, total, picked), "fsdp", combine_totals)
    highest = lax.dynamic_slice_in_dim(highest, own_start, tok_rows, 0)
    total = lax.dynamic_slice_in_dim(total, own_start, tok_rows, 0)
    picked = lax.dynamic_slice_in_dim(picked, own_start, tok_rows, 0)
    new_logprob = picked - (highest + jnp.log(total))
    position = shard_pos % 2 * tok_rows + jnp.arange(tok_rows, dtype=jnp.int32)
    limit = lax.dynamic_index_in_dim(lengths[0], shard_pos // 2, 0, keepdims=False)
    live = position < limit
    log_ratio = jnp.where(live, new_logprob - old_logprob, jnp.float32(0.0))
    gap = jnp.clip(old_logprob - new_logprob, -3.0, 3.0)
    kl_term = jnp.where(live, jnp.exp(gap) - gap - 1.0, jnp.float32(0.0))
    return (log_ratio, kl_term)


def solution(mesh):
    return jax.shard_map(
        on_device,
        mesh=mesh,
        in_specs=(
            P(("dp", "fsdp"), None),
            P(None, "dp", "fsdp", None),
            P(("dp", "fsdp"), None),
            P(None, "fsdp"),
            P(),
            P("fsdp", None),
            P(),
            P("dp", None),
            P(("dp", "fsdp")),
            P(("dp", "fsdp")),
        ),
        out_specs=(P(("dp", "fsdp")), P(("dp", "fsdp"))),
        check_vma=False,
    )
```

profile of v0, /device:TPU:1, one launch (start us, length us, event | category | flops | bytes accessed | tf_op | source)
XLA Modules:
  0.0 398.0 jit_solution(15612936221681823901)
XLA Ops:
  7.2 0.0 copy-start
  7.2 0.0 all-gather.10.cloned.1.call-start
  7.2 1.9 copy.19
  9.2 0.0 all-gather.10.cloned.1.call-update
  9.2 0.0 all-gather.16.cloned.1.call-start
  9.2 1.2 dynamic_slice.31
  12.4 54.9 %all-gather.10.cloned.1.call-done = bf16[2,8,32,2048]{3,0,1,2:T(2,128)(2,1)} async-done(((bf16[2,1,32,2048]{3,0,1,2:T(2,128)(2,1)}), bf16[2,8,32,2048]{3,0,1,2:T(2,128)(2,1)}) %all-gather.10.cloned.1.call-update) | async-done | bytes 2097168 | tf_op jit(solution)/shard_map/all_gather | solution.py:46
  67.3 1.8 constant_dynamic-slice_fusion.3
  69.2 0.0 all-gather.16.cloned.1.call-update
  69.2 0.0 all-gather.12.cloned.1.call-start
  69.3 0.7 all-gather.12.cloned.1.call-update
  69.9 0.0 all-gather.14.cloned.1.call-start
  70.0 35.5 %all-gather.16.cloned.1.call-done = bf16[2,1,512,2048]{3,0,1,2:T(2,128)(2,1)} async-done(((bf16[2,1,32,2048]{3,0,1,2:T(2,128)(2,1)}), bf16[2,1,512,2048]{3,0,1,2:T(2,128)(2,1)}) %all-gather.16.cloned.1.call-update) | async-done | bytes 4194320 | tf_op jit(solution)/shard_map/all_gather | solution.py:48
  105.5 10.3 %fusion.19 = (bf16[1,1,512,2048]{3,0,1,2:T(2,128)(2,1)}, bf16[1,1,512,2048]{3,0,1,2:T(2,128)(2,1)}) fusion(bf16[2,1,512,2048]{3,0,1,2:T(2,128)(2,1)} %all-gather.16.cloned.1.call-done), kind=kLoop, calls=%fused_computation.34 | loop fusion | bytes 8388608 | tf_op jit(solution)/shard_map/slice | solution.py:49
  115.8 9.1 %copy.27 = bf16[1,1,512,2048]{2,3,1,0:T(8,128)(2,1)S(1)} copy(bf16[1,1,512,2048]{3,0,1,2:T(2,128)(2,1)} %get-tuple-element.66) | data formatting | bytes 4194304
  125.0 0.0 copy-start.5
  125.0 10.7 %copy.20 = bf16[1,1,512,2048]{2,3,1,0:T(8,128)(2,1)} copy(bf16[1,1,512,2048]{3,0,1,2:T(2,128)(2,1)} %get-tuple-element.67) | data formatting | bytes 4194304 | tf_op jit(solution)/shard_map/slice | solution.py:49
  135.7 0.0 copy-done.5
  135.7 0.8 fusion.7
  136.6 0.0 copy-start.3
  136.6 1.3 copy-done.3
  137.9 0.0 copy-start.2
  137.9 0.6 fusion.20
  138.4 1.0 copy-done.2
  139.5 4.3 %convolution_convert_fusion = bf16[8,256,128]{2,1,0:T(8,128)(2,1)} fusion(bf16[512,8,256]{0,2,1:T(8,128)(2,1)S(1)} %bitcast.48, f32[8,128]{1,0:T(8,128)S(1)} %fusion.20, f32[8,512,128]{2,1,0:T(8,128)} %copy-done.3), kind=kOutput, calls=%fused_computation.16 | convolution fusion | flops 271320576 | bytes 4722688 | tf_op jit(solution)/shard_map/htl,lhd->thd/dot_general | solution.py:30
  143.7 63.0 %all-gather.12.cloned.1.call-done = bf16[2048,4096]{1,0:T(8,128)(2,1)} async-done(((bf16[2048,256]{1,0:T(8,128)(2,1)}), bf16[2048,4096]{1,0:T(8,128)(2,1)}) %all-gather.12.cloned.1.call-update) | async-done | bytes 16777232 | tf_op jit(solution)/shard_map/all_gather | solution.py:52
  206.7 0.0 copy-done.4
  206.7 8.6 %multiply_reduce_fusion = (f32[128]{0:T(128)S(1)}, f32[128,4096]{1,0:T(8,128)S(1)}) fusion(bf16[128,4096]{1,0:T(8,128)(2,1)S(1)} %copy-done.4, bf16[128,2048]{0,1:T(8,128)(2,1)} %bitcast.52, bf16[2048,4096]{1,0:T(8,128)(2,1)} %all-gather.12.cloned.1.call-done), kind=kOutput, calls=%fused_computation.13 | convolution fusion | flops 2149580800 | bytes 20447744 | tf_op jit(solution)/shard_map/dot_general | solution.py:50
  215.3 0.0 copy-done.6
  215.3 0.0 copy-start.8
  215.3 1.3 multiply_convert_fusion
  216.6 0.0 all-gather.14.cloned.1.call-update
  216.6 0.0 copy-done
  216.6 0.6 constant_dynamic-slice_fusion.4
  217.3 0.0 copy-done.8
  217.3 17.7 %all-gather.4 = s32[16,1,128]{2,1,0:T(1,128)S(1)} all-gather(s32[1,1,128]{2,1,0:T(1,128)S(1)} %bitcast.55), channel_id=1, replica_groups=mesh['dp'=8,'fsdp'=16] {'fsdp'}, dimensions={0}, use_global_device_ids=true | all-gather | bytes 8704 | tf_op jit(solution)/shard_map/all_gather | solution.py:60
  235.0 73.2 %all-gather.14.cloned.1.call-done = bf16[2048,4096]{1,0:T(8,128)(2,1)} async-done(((bf16[128,4096]{1,0:T(8,128)(2,1)}), bf16[2048,4096]{1,0:T(8,128)(2,1)}) %all-gather.14.cloned.1.call-update) | async-done | bytes 16777232 | tf_op jit(solution)/shard_map/all_gather | solution.py:59
  308.2 22.8 %fusion.21 = (f32[2048]{0:T(1024)S(1)}, f32[2048,1024]{0,1:T(8,128)S(1)}) fusion(bf16[2048,4096]{1,0:T(8,128)(2,1)} %all-gather.14.cloned.1.call-done, bf16[1024,4096]{1,0:T(8,128)(2,1)} %param.17), kind=kOutput, calls=%fused_computation.36 | convolution fusion | flops 17181964288 | bytes 33562624 | tf_op jit(solution)/shard_map/dot_general | solution.py:63
  331.0 19.4 %all-gather.1 = f32[32768]{0:T(1024)S(1)} all-gather(f32[2048]{0:T(1024)S(1)} %get-tuple-element.70), channel_id=3, replica_groups=mesh['dp'=8,'fsdp'=16] {'fsdp'}, dimensions={0}, use_global_device_ids=true | all-gather | bytes 139264 | tf_op jit(solution)/shard_map/all_gather | solution.py:10
  350.5 2.5 select_reduce_fusion
  352.9 0.0 copy-start.7
  352.9 16.6 %all-gather.2 = f32[32768]{0:T(1024)S(1)} all-gather(f32[2048]{0:T(1024)S(1)} %get-tuple-element.45), channel_id=4, replica_groups=mesh['dp'=8,'fsdp'=16] {'fsdp'}, dimensions={0}, use_global_device_ids=true | all-gather | bytes 139264 | tf_op jit(solution)/shard_map/all_gather | solution.py:10
  369.6 17.9 %all-gather.3 = f32[32768]{0:T(1024)S(1)} all-gather(f32[2048]{0:T(1024)S(1)} %get-tuple-element.44), channel_id=5, replica_groups=mesh['dp'=8,'fsdp'=16] {'fsdp'}, dimensions={0}, use_global_device_ids=true | all-gather | bytes 139264 | tf_op jit(solution)/shard_map/all_gather | solution.py:10
  387.6 1.5 while.14
  389.1 0.0 copy-done.7
  389.1 1.2 compare_select_fusion
  390.4 1.1 compare_select_fusion.1
  391.5 0.0 copy-done.1
  (74 shorter events, 0.9 us)
Async XLA Ops:
  7.2 209.5 %copy-start = (s32[1,8]{1,0:T(1,128)S(1)}, s32[1,8]{1,0:T(1,128)}, u32[]{:S(2)}) copy-start(s32[1,8]{1,0:T(1,128)} %param.19) | copy-start | bytes 100
  7.2 60.2 %all-gather.10.cloned.1.call-start = ((), (), s32[]{:S(2)}) async-start(), calls=%async_computation | async-start | bytes 2359296 | tf_op jit(solution)/shard_map/all_gather | solution.py:46
  9.2 96.4 %all-gather.16.cloned.1.call-start = ((), (), s32[]{:S(2)}) async-start(), calls=%async_computation.3 | async-start | bytes 4456448 | tf_op jit(solution)/shard_map/all_gather | solution.py:48
  69.2 137.5 %all-gather.12.cloned.1.call-start = ((), (), s32[]{:S(2)}) async-start(), calls=%async_computation.1 | async-start | bytes 17825792 | tf_op jit(solution)/shard_map/all_gather | solution.py:52
  69.9 238.3 %all-gather.14.cloned.1.call-start = ((), (), s32[]{:S(2)}) async-start(), calls=%async_computation.2 | async-start | bytes 17825792 | tf_op jit(solution)/shard_map/all_gather | solution.py:59
  125.0 10.7 %copy-start.5 = (bf16[128,2048]{1,0:T(8,128)(2,1)S(1)}, bf16[128,2048]{1,0:T(8,128)(2,1)}, u32[]{:S(2)}) copy-start(bf16[128,2048]{1,0:T(8,128)(2,1)} %param.12) | copy-start | bytes 1572868
  136.6 1.3 copy-start.3
  137.9 1.6 copy-start.2
  139.5 67.2 %copy-start.4 = (bf16[128,4096]{1,0:T(8,128)(2,1)S(1)}, bf16[128,4096]{1,0:T(8,128)(2,1)}, u32[]{:S(2)}) copy-start(bf16[128,4096]{1,0:T(8,128)(2,1)} %param.14) | copy-start | bytes 3145732
  206.7 8.6 %copy-start.6 = (f32[4096]{0:T(1024)S(1)}, f32[4096]{0:T(1024)}, u32[]{:S(2)}) copy-start(f32[4096]{0:T(1024)} %param.16) | copy-start | bytes 49156
  215.3 2.0 copy-start.8
  350.5 41.1 %copy-start.1 = (s32[1,8]{1,0:T(1,128)S(1)}, s32[1,8]{1,0:T(1,128)}, u32[]{:S(2)}) copy-start(s32[1,8]{1,0:T(1,128)} %param.19) | copy-start | bytes 100
  352.9 36.2 %copy-start.7 = (f32[128]{0:T(128)S(1)}, f32[128]{0:T(128)}, u32[]{:S(2)}) copy-start(f32[128]{0:T(128)} %param.21) | copy-start | bytes 1540
Sparse Core Ops, SparseCore 0:
  10.2 57.1 all-gather.9
  69.3 36.1 all-gather.15
  107.2 99.4 all-gather.11
  216.7 91.4 all-gather.13
where the time goes:
time: 399 us; the launch traced here: 398 us
  waiting for transfers between devices  227 us (57%)
  blocking collectives  71.7 us (18%)
  local copies, waits for them, and re-layouts  38.8 us (10%)
  matrix products  36.5 us (9%)
  between operations  15.9 us (4%)
  other arithmetic  6.93 us (2%)
    all_gather x1, waiting for transfers between devices, on_device(): lax.all_gather(hidden, 'fsdp', axis=0, tiled=True)  73.2 us
    all_gather x1, waiting for transfers between devices, on_device(): lax.all_gather(out_weight, 'fsdp', axis=1, tiled=True)  63 us
    all_gather x1, waiting for transfers between devices, on_device(): every_doc = lax.all_gather(doc_kv, 'dp', axis=1, tiled=True)  54.9 us
    all_gather x3, blocking collectives, joined(): pieces = jax.tree.map(lambda part: lax.all_gather(part, axis), value)  54 us
    all_gather x1, waiting for transfers between devices, on_device(): whole_doc = lax.all_gather(chosen, 'fsdp', axis=1, tiled=True)  35.5 us
    dot_general x1, matrix products, on_device(): lax.dot_general(group_hidden, head, (((1,), (1,)), ((), ())), preferred_e...  22.8 us
    slice x2, local copies, waits for them, and re-layouts, on_device(): attended = attend(queries, whole_doc[0], whole_doc[1], HEADS)  21 us
    all_gather x1, blocking collectives, on_device(): lax.all_gather(sampled, 'fsdp', axis=0, tiled=True)  17.7 us
  transfers between devices with their start and end apart: 4, of which 4 were waited for; matrix products, arithmetic and copies ran while one was open for 9% of the time, Pallas kernels for 0%

commit v1 on v0

--- a/solution.py
+++ b/solution.py
@@ -4,6 +4,12 @@
 from jax.sharding import PartitionSpec as P
 
 HEADS = 8
+find_shifts_all_in = lambda work_x, d_out: jnp.concatenate(
+    lax.all_to_all(
+        jnp.stack([work_x] * lax.axis_size("fsdp")), axis_name="fsdp", split_axis=0, concat_axis=0
+    ),
+    axis=d_out,
+)
 
 
 def joined(value, axis, join):
@@ -47,11 +53,7 @@
     chosen = lax.dynamic_index_in_dim(every_doc, source[row_pos], 1, keepdims=False)
     whole_doc = lax.all_gather(chosen, "fsdp", axis=1, tiled=True)
     attended = attend(queries, whole_doc[0], whole_doc[1], HEADS)
-    mixed = jnp.dot(
-        attended,
-        lax.all_gather(out_weight, "fsdp", axis=1, tiled=True),
-        preferred_element_type=jnp.float32,
-    )
+    mixed = jnp.dot(attended, find_shifts_all_in(out_weight, 1), preferred_element_type=jnp.float32)
     summed = mixed + residual.astype(jnp.float32)
     scale = lax.rsqrt(jnp.mean(summed * summed, axis=1, keepdims=True) + 1e-06)
     hidden = (summed * scale * out_gain[None, :]).astype(jnp.bfloat16)

time: 399 us -> 495 us (1.24)
  waiting for transfers between devices: 227 us -> 302 us
  starting transfers between devices: 0.16 us -> 8.01 us
  local copies, waits for them, and re-layouts: 38.8 us -> 44 us
  blocking collectives: 71.7 us -> 76.8 us
    all_gather x1, waiting for transfers between devices: 35.5 us -> 123 us  [on_device(): whole_doc = lax.all_gather(chosen, 'fsdp', axis=1, tiled=True)]
    all_gather x1 -> x0, waiting for transfers between devices: 63 us -> none  [on_device(): lax.all_gather(out_weight, 'fsdp', axis=1, tiled=True)]
    all_to_all x0 -> x1, waiting for transfers between devices: none -> 36.6 us  [lax.all_to_all(jnp.stack([work_x] * lax.axis_size('fsdp')), axis_name='fs...]
    all_gather x1, waiting for transfers between devices: 54.9 us -> 69.1 us  [on_device(): every_doc = lax.all_gather(doc_kv, 'dp', axis=1, tiled=True)]
    all_to_all x0 -> x1, starting transfers between devices: none -> 7.89 us  [lax.all_to_all(jnp.stack([work_x] * lax.axis_size('fsdp')), axis_name='fs...]
    another operation x0 -> x1, local copies, waits for them, and re-layouts: none -> 5.99 us  [jnp.stack([work_x] * lax.axis_size('fsdp'))]
    all_gather x1, blocking collectives: 17.7 us -> 22.8 us  [on_device(): lax.all_gather(sampled, 'fsdp', axis=0, tiled=True)]
    unnamed x20 -> x25, local copies, waits for them, and re-layouts: 13.4 us -> 13.9 us
  transfers between devices with their start and end apart: 4 -> 4, of which waited for: 4 -> 4; matrix products, arithmetic and copies ran while one was open for 9% -> 8% of each run, Pallas kernels for 0% -> 0%
where the time goes in v1:
time: 495 us; the launch traced here: 494 us
  waiting for transfers between devices  302 us (61%)
  blocking collectives  76.8 us (16%)
  local copies, waits for them, and re-layouts  44 us (9%)
  matrix products  39.6 us (8%)
  between operations  15.9 us (3%)
  starting transfers between devices  8.01 us (2%)
  other arithmetic  6.93 us (1%)
    all_gather x1, waiting for transfers between devices, on_device(): whole_doc = lax.all_gather(chosen, 'fsdp', axis=1, tiled=True)  123 us
    all_gather x1, waiting for transfers between devices, on_device(): lax.all_gather(hidden, 'fsdp', axis=0, tiled=True)  73.4 us
    all_gather x1, waiting for transfers between devices, on_device(): every_doc = lax.all_gather(doc_kv, 'dp', axis=1, tiled=True)  69.1 us
    all_gather x3, blocking collectives, joined(): pieces = jax.tree.map(lambda part: lax.all_gather(part, axis), value)  54 us
    all_to_all x1, waiting for transfers between devices, lax.all_to_all(jnp.stack([work_x] * lax.axis_size('fsdp')), axis_name='fs...  36.6 us
    dot_general x1, matrix products, on_device(): lax.dot_general(group_hidden, head, (((1,), (1,)), ((), ())), preferred_e...  22.8 us
    all_gather x1, blocking collectives, on_device(): lax.all_gather(sampled, 'fsdp', axis=0, tiled=True)  22.8 us
    slice x2, local copies, waits for them, and re-layouts, on_device(): attended = attend(queries, whole_doc[0], whole_doc[1], HEADS)  20.5 us
  transfers between devices with their start and end apart: 4, of which 4 were waited for; matrix products, arithmetic and copies ran while one was open for 8% of the time, Pallas kernels for 0%

profile of v1, /device:TPU:1, one launch (start us, length us, event | category | flops | bytes accessed | tf_op | source)
XLA Modules:
  0.0 494.1 jit_solution(13651926902195945142)
XLA Ops:
  7.2 0.0 copy-start
  7.2 1.5 copy.26
  8.7 6.0 %stack.2 = bf16[16,2048,256]{1,2,0:T(8,128)(2,1)} broadcast(bf16[2048,256]{0,1:T(8,128)(2,1)S(1)} %copy.26), dimensions={1,2} | broadcast | bytes 17825792 | tf_op jit(solution)/shard_map/stack | solution.py:9
  14.7 7.9 %all-to-all-start = ((bf16[16,2048,256]{1,2,0:T(8,128)(2,1)}), bf16[16,2048,256]{1,2,0:T(8,128)(2,1)}, u32[]{:S(2)}, u32[]{:S(2)}) async-start(bf16[16,2048,256]{1,2,0:T(8,128)(2,1)} %stack.2), calls=%async_computation | async-start | bytes 33554432 | tf_op jit(solution)/shard_map/all_to_all | solution.py:8
  22.6 0.0 all-gather.9.cloned.1.call-start
  22.6 0.0 copy-done.6
  22.6 1.0 copy.20
  23.6 0.0 all-gather.9.cloned.1.call-update
  23.6 0.0 all-gather.13.cloned.1.call-start
  23.7 0.0 copy-done.10
  23.7 0.6 dynamic_slice.31
  26.2 69.1 %all-gather.9.cloned.1.call-done = bf16[2,8,32,2048]{3,0,1,2:T(2,128)(2,1)} async-done(((bf16[2,1,32,2048]{3,0,1,2:T(2,128)(2,1)}), bf16[2,8,32,2048]{3,0,1,2:T(2,128)(2,1)}) %all-gather.9.cloned.1.call-update) | async-done | bytes 2097168 | tf_op jit(solution)/shard_map/all_gather | solution.py:52
  95.3 1.8 constant_dynamic-slice_fusion.3
  97.2 0.0 all-gather.13.cloned.1.call-update
  97.2 0.0 all-gather.11.cloned.1.call-start
  97.2 123.0 %all-gather.13.cloned.1.call-done = bf16[2,1,512,2048]{3,0,1,2:T(2,128)(2,1)} async-done(((bf16[2,1,32,2048]{3,0,1,2:T(2,128)(2,1)}), bf16[2,1,512,2048]{3,0,1,2:T(2,128)(2,1)}) %all-gather.13.cloned.1.call-update) | async-done | bytes 4194320 | tf_op jit(solution)/shard_map/all_gather | solution.py:54
  220.3 10.0 %fusion.19 = (bf16[1,1,512,2048]{3,0,1,2:T(2,128)(2,1)}, bf16[1,1,512,2048]{3,0,1,2:T(2,128)(2,1)}) fusion(bf16[2,1,512,2048]{3,0,1,2:T(2,128)(2,1)} %all-gather.13.cloned.1.call-done), kind=kLoop, calls=%fused_computation.34 | loop fusion | bytes 8388608 | tf_op jit(solution)/shard_map/slice | solution.py:55
  230.2 9.0 %copy.29 = bf16[1,1,512,2048]{2,3,1,0:T(8,128)(2,1)S(1)} copy(bf16[1,1,512,2048]{3,0,1,2:T(2,128)(2,1)} %get-tuple-element.66) | data formatting | bytes 4194304
  239.2 0.0 copy-start.5
  239.2 10.5 %copy.21 = bf16[1,1,512,2048]{2,3,1,0:T(8,128)(2,1)} copy(bf16[1,1,512,2048]{3,0,1,2:T(2,128)(2,1)} %get-tuple-element.67) | data formatting | bytes 4194304 | tf_op jit(solution)/shard_map/slice | solution.py:55
  249.7 0.0 copy-done.5
  249.7 0.8 fusion.7
  250.6 0.0 copy-start.3
  250.6 1.4 copy-done.3
  252.0 0.6 fusion.20
  252.6 1.0 copy-done.2
  253.6 4.3 convolution_convert_fusion
  257.9 36.6 %all-to-all-done = bf16[16,2048,256]{1,2,0:T(8,128)(2,1)} async-done(((bf16[16,2048,256]{1,2,0:T(8,128)(2,1)}), bf16[16,2048,256]{1,2,0:T(8,128)(2,1)}, u32[]{:S(2)}, u32[]{:S(2)}) %all-to-all-start) | async-done | bytes 16777248 | tf_op jit(solution)/shard_map/all_to_all | solution.py:8
  294.5 0.0 copy-done.4
  294.5 11.7 %multiply_reduce_fusion = (f32[128]{0:T(128)S(1)}, f32[128,4096]{1,0:T(8,128)S(1)}) fusion(bf16[128,4096]{1,0:T(8,128)(2,1)S(1)} %copy-done.4, bf16[128,2048]{0,1:T(8,128)(2,1)} %bitcast.56, bf16[2048,4096]{0,1:T(8,128)(2,1)} %bitcast.11), kind=kOutput, calls=%fused_computation.13 | convolution fusion | flops 2149580800 | bytes 20447744 | tf_op jit(solution)/shard_map/dot_general | solution.py:56
  306.1 0.0 copy-done.7
  306.1 0.0 copy-start.9
  306.1 1.3 multiply_convert_fusion
  307.4 0.0 all-gather.11.cloned.1.call-update
  307.4 0.0 copy-done
  307.5 0.6 constant_dynamic-slice_fusion.4
  308.1 0.0 copy-done.9
  308.1 22.8 %all-gather.4 = s32[16,1,128]{2,1,0:T(1,128)S(1)} all-gather(s32[1,1,128]{2,1,0:T(1,128)S(1)} %bitcast.58), channel_id=1, replica_groups=mesh['dp'=8,'fsdp'=16] {'fsdp'}, dimensions={0}, use_global_device_ids=true | all-gather | bytes 8704 | tf_op jit(solution)/shard_map/all_gather | solution.py:62
  330.8 73.4 %all-gather.11.cloned.1.call-done = bf16[2048,4096]{1,0:T(8,128)(2,1)} async-done(((bf16[128,4096]{1,0:T(8,128)(2,1)}), bf16[2048,4096]{1,0:T(8,128)(2,1)}) %all-gather.11.cloned.1.call-update) | async-done | bytes 16777232 | tf_op jit(solution)/shard_map/all_gather | solution.py:61
  404.3 22.8 %fusion.21 = (f32[2048]{0:T(1024)S(1)}, f32[2048,1024]{0,1:T(8,128)S(1)}) fusion(bf16[2048,4096]{1,0:T(8,128)(2,1)} %all-gather.11.cloned.1.call-done, bf16[1024,4096]{1,0:T(8,128)(2,1)} %param.17), kind=kOutput, calls=%fused_computation.36 | convolution fusion | flops 17181964288 | bytes 33562624 | tf_op jit(solution)/shard_map/dot_general | solution.py:65
  427.1 19.4 %all-gather.1 = f32[32768]{0:T(1024)S(1)} all-gather(f32[2048]{0:T(1024)S(1)} %get-tuple-element.70), channel_id=3, replica_groups=mesh['dp'=8,'fsdp'=16] {'fsdp'}, dimensions={0}, use_global_device_ids=true | all-gather | bytes 139264 | tf_op jit(solution)/shard_map/all_gather | solution.py:16
  446.5 2.5 select_reduce_fusion
  449.0 0.0 copy-start.8
  449.0 16.6 %all-gather.2 = f32[32768]{0:T(1024)S(1)} all-gather(f32[2048]{0:T(1024)S(1)} %get-tuple-element.45), channel_id=4, replica_groups=mesh['dp'=8,'fsdp'=16] {'fsdp'}, dimensions={0}, use_global_device_ids=true | all-gather | bytes 139264 | tf_op jit(solution)/shard_map/all_gather | solution.py:16
  465.6 17.9 %all-gather.3 = f32[32768]{0:T(1024)S(1)} all-gather(f32[2048]{0:T(1024)S(1)} %get-tuple-element.44), channel_id=5, replica_groups=mesh['dp'=8,'fsdp'=16] {'fsdp'}, dimensions={0}, use_global_device_ids=true | all-gather | bytes 139264 | tf_op jit(solution)/shard_map/all_gather | solution.py:16
  483.7 1.5 while.14
  485.2 1.2 compare_select_fusion
  486.5 1.1 compare_select_fusion.1
  (79 shorter events, 0.9 us)
Async XLA Ops:
  7.2 300.3 %copy-start = (s32[1,8]{1,0:T(1,128)S(1)}, s32[1,8]{1,0:T(1,128)}, u32[]{:S(2)}) copy-start(s32[1,8]{1,0:T(1,128)} %param.19) | copy-start | bytes 100
  14.7 7.9 %copy-start.6 = (bf16[2,1,32,2048]{3,2,1,0:T(8,128)(2,1)S(1)}, bf16[2,1,32,2048]{3,2,1,0:T(8,128)(2,1)}, u32[]{:S(2)}) copy-start(bf16[2,1,32,2048]{3,2,1,0:T(8,128)(2,1)} %param.13) | copy-start | bytes 786436
  14.7 9.0 %copy-start.10 = (s32[8]{0:T(128)S(1)}, s32[8]{0:T(128)}, u32[]{:S(2)}) copy-start(s32[8]{0:T(128)} %param.18) | copy-start | bytes 100
  14.7 279.8 %all-to-all-start = ((bf16[16,2048,256]{1,2,0:T(8,128)(2,1)}), bf16[16,2048,256]{1,2,0:T(8,128)(2,1)}, u32[]{:S(2)}, u32[]{:S(2)}) async-start(bf16[16,2048,256]{1,2,0:T(8,128)(2,1)} %stack.2), calls=%async_computation | async-start | bytes 33554432 | tf_op jit(solution)/shard_map/all_to_all | solution.py:8
  22.6 72.8 %all-gather.9.cloned.1.call-start = ((), (), s32[]{:S(2)}) async-start(), calls=%async_computation.1 | async-start | bytes 2359296 | tf_op jit(solution)/shard_map/all_gather | solution.py:52
  23.6 196.7 %all-gather.13.cloned.1.call-start = ((), (), s32[]{:S(2)}) async-start(), calls=%async_computation.3 | async-start | bytes 4456448 | tf_op jit(solution)/shard_map/all_gather | solution.py:54
  97.2 307.1 %all-gather.11.cloned.1.call-start = ((), (), s32[]{:S(2)}) async-start(), calls=%async_computation.2 | async-start | bytes 17825792 | tf_op jit(solution)/shard_map/all_gather | solution.py:61
  239.2 10.5 %copy-start.5 = (bf16[128,2048]{1,0:T(8,128)(2,1)S(1)}, bf16[128,2048]{1,0:T(8,128)(2,1)}, u32[]{:S(2)}) copy-start(bf16[128,2048]{1,0:T(8,128)(2,1)} %param.12) | copy-start | bytes 1572868
  250.6 1.4 copy-start.3
  252.0 1.6 copy-start.2
  253.6 40.9 %copy-start.4 = (bf16[128,4096]{1,0:T(8,128)(2,1)S(1)}, bf16[128,4096]{1,0:T(8,128)(2,1)}, u32[]{:S(2)}) copy-start(bf16[128,4096]{1,0:T(8,128)(2,1)} %param.14) | copy-start | bytes 3145732
  294.5 11.7 %copy-start.7 = (f32[4096]{0:T(1024)S(1)}, f32[4096]{0:T(1024)}, u32[]{:S(2)}) copy-start(f32[4096]{0:T(1024)} %param.16) | copy-start | bytes 49156
  306.1 1.9 copy-start.9
  446.5 41.1 %copy-start.1 = (s32[1,8]{1,0:T(1,128)S(1)}, s32[1,8]{1,0:T(1,128)}, u32[]{:S(2)}) copy-start(s32[1,8]{1,0:T(1,128)} %param.19) | copy-start | bytes 100
  449.0 36.2 %copy-start.8 = (f32[128]{0:T(128)S(1)}, f32[128]{0:T(128)}, u32[]{:S(2)}) copy-start(f32[128]{0:T(128)} %param.21) | copy-start | bytes 1540
Sparse Core Ops, SparseCore 0:
  25.6 69.7 all-gather.8
  97.3 122.9 all-gather.12
  307.5 96.6 all-gather.10
